TPU v7x, 32 devices: a whole 2x2x4 slice. The times are simulated.
32 devices in a mesh: grp: 8 (over z, y), seq: 4 (over x, core).
Axes of the slice: x: 2, y: 2, z: 4, core: 2. Of those that a mesh axis runs over, the one named last changes fastest.
Arguments:
- tokens_in: bfloat16 [24576, 768], P(('grp', 'seq')), may hold values from -6 to 6
- lengths: int32 [8], P('grp'), may hold values from 2305 to 3072, as said below
- ln1_gain: float32 [768], replicated, may hold values from 0.5 to 1.5
- ln1_bias: float32 [768], replicated, may hold values from -1.75 to 1.75
- w_qkv: bfloat16 [768, 2304], replicated, may hold values from -0.21875 to 0.21875
- bias_query: float32 [768], replicated, may hold values from -1.75 to 1.75
- bias_value: float32 [768], replicated, may hold values from -1.75 to 1.75
- w_out: bfloat16 [768, 768], replicated, may hold values from -0.875 to 0.875
- bias_out: float32 [768], replicated, may hold values from -1.75 to 1.75
- ln2_gain: float32 [768], replicated, may hold values from 0.5 to 1.5
- ln2_bias: float32 [768], replicated, may hold values from -1.75 to 1.75
- w_up: bfloat16 [768, 3072], replicated, may hold values from -0.21875 to 0.21875
- bias_up: float32 [3072], replicated, may hold values from -1.75 to 1.75
- w_down: bfloat16 [3072, 768], replicated, may hold values from -0.109375 to 0.109375
- bias_down: float32 [768], replicated, may hold values from -1.75 to 1.75
- proj_patch: bfloat16 [768, 768], replicated, may hold values from -0.21875 to 0.21875
- proj_class: bfloat16 [768, 768], replicated, may hold values from -0.21875 to 0.21875
- class_emb: bfloat16 [150, 768], replicated, may hold values from -6 to 6
- d_masks: bfloat16 [24576, 150], P(('grp', 'seq')), may hold values from -6 to 6
Outputs:
- masks: bfloat16 [24576, 150], P(('grp', 'seq'))
- grad_tokens: bfloat16 [24576, 768], P(('grp', 'seq'))
- grad_ln1_gain: float32 [768], P('grp')
- grad_ln1_bias: float32 [768], P('grp')
- grad_w_qkv: float32 [768, 2304], P('grp', 'seq')
- grad_bias_query: float32 [768], P('grp')
- grad_bias_value: float32 [768], P('grp')
- grad_w_out: float32 [768, 768], P('grp', 'seq')
- grad_bias_out: float32 [768], P('grp')
- grad_ln2_gain: float32 [768], P('grp')
- grad_ln2_bias: float32 [768], P('grp')
- grad_w_up: float32 [768, 3072], P('grp', 'seq')
- grad_bias_up: float32 [3072], P('grp')
- grad_w_down: float32 [3072, 768], P('grp', 'seq')
- grad_bias_down: float32 [768], P('grp')
- grad_proj_patch: float32 [768, 768], P('grp', 'seq')
- grad_proj_class: float32 [768, 768], P('grp', 'seq')
- grad_class_emb: float32 [150, 768], P(None, 'grp')
Inputs may be any that keep to these rules, and one draw needn't show every extreme that they name: Image g fills the first lengths[g] rows of its 3072 rows, the rest is padding; in every draw some image has exactly 3072 rows.
All inputs are finite; a program needn't handle non-finite values.
Results may differ from a plain program's by a relative error of at most 0.015.
Values may be sent and summed in bfloat16 or wider, within the bound.
A program may use at most 256 MiB of HBM per device.

v0:
```python
import math
import jax
import jax.numpy as jnp
from jax import lax
from jax.sharding import PartitionSpec as P

HEAD_DIM = 64
EPS_NORM = 1e-06
EPS_UNIT = 1e-06
NEG_FILL = -1e30


def layer_norm(matrix_rows, gain_vec, shift_vec):
    row_mean = jnp.mean(matrix_rows, axis=-1, keepdims=True)
    centred = matrix_rows - row_mean
    row_var = jnp.mean(centred * centred, axis=-1, keepdims=True)
    return centred * lax.rsqrt(row_var + EPS_NORM) * gain_vec + shift_vec


def unit_rows(matrix_rows):
    return matrix_rows * lax.rsqrt(
        jnp.sum(matrix_rows * matrix_rows, axis=-1, keepdims=True) + EPS_UNIT
    )


def gelu_exact(values_in):
    return jax.nn.gelu(values_in, approximate=False)


def score_block(query_heads, key_block, keep_block, score_scale):
    scores = (
        jnp.einsum("qhd,khd->hqk", query_heads, key_block, preferred_element_type=jnp.float32)
        * score_scale
    )
    return jnp.where(keep_block[None, None, :], scores, NEG_FILL)


def split_blocks(key_heads, value_heads, key_keep, key_span):
    block_count = key_heads.shape[0] // key_span
    head_count = key_heads.shape[1]
    key_blocks = key_heads.reshape(block_count, key_span, head_count, -1)
    value_blocks = value_heads.reshape(block_count, key_span, head_count, -1)
    keep_blocks = key_keep.reshape(block_count, key_span)
    return (key_blocks, value_blocks, keep_blocks)


def attend_forward(query_heads, key_heads, value_heads, key_keep, score_scale, key_span):
    row_count, head_count = (query_heads.shape[0], query_heads.shape[1])
    key_blocks, value_blocks, keep_blocks = split_blocks(key_heads, value_heads, key_keep, key_span)

    def gather_stats(carried, pieces):
        row_top, row_total = carried
        key_block, keep_block = pieces
        scores = score_block(query_heads, key_block, keep_block, score_scale)
        new_top = jnp.maximum(row_top, jnp.max(scores, axis=-1))
        row_total = row_total * jnp.exp(row_top - new_top) + jnp.sum(
            jnp.exp(scores - new_top[..., None]), axis=-1
        )
        return ((new_top, row_total), None)

    start_stats = (
        jnp.full((head_count, row_count), NEG_FILL, jnp.float32),
        jnp.zeros((head_count, row_count), jnp.float32),
    )
    row_top, row_total = lax.scan(gather_stats, start_stats, (key_blocks, keep_blocks))[0]
    log_mass = row_top + jnp.log(row_total)

    def weigh_values(summed, pieces):
        key_block, value_block, keep_block = pieces
        scores = score_block(query_heads, key_block, keep_block, score_scale)
        prob_low = jnp.exp(scores - log_mass[..., None]).astype(jnp.bfloat16)
        summed = summed + jnp.einsum(
            "hqk,khd->qhd", prob_low, value_block, preferred_element_type=jnp.float32
        )
        return (summed, None)

    start_sum = jnp.zeros(query_heads.shape, jnp.float32)
    attended = lax.scan(weigh_values, start_sum, (key_blocks, value_blocks, keep_blocks))[0]
    return (attended, log_mass)


def attend_backward(
    query_heads,
    key_heads,
    value_heads,
    key_keep,
    grad_heads,
    log_mass,
    attended,
    score_scale,
    key_span,
):
    head_count = query_heads.shape[1]
    key_blocks, value_blocks, keep_blocks = split_blocks(key_heads, value_heads, key_keep, key_span)
    row_delta = jnp.einsum("qhd,qhd->hq", grad_heads.astype(jnp.float32), attended)

    def spread_grads(grad_query, pieces):
        key_block, value_block, keep_block = pieces
        prob_rows = jnp.exp(
            score_block(query_heads, key_block, keep_block, score_scale) - log_mass[..., None]
        )
        grad_probs = jnp.einsum(
            "qhd,khd->hqk", grad_heads, value_block, preferred_element_type=jnp.float32
        )
        grad_scores = (prob_rows * (grad_probs - row_delta[..., None])).astype(jnp.bfloat16)
        grad_query = grad_query + jnp.einsum(
            "hqk,khd->qhd", grad_scores, key_block, preferred_element_type=jnp.float32
        )
        grad_key_block = (
            jnp.einsum("hqk,qhd->khd", grad_scores, query_heads, preferred_element_type=jnp.float32)
            * score_scale
        )
        grad_value_block = jnp.einsum(
            "hqk,qhd->khd",
            prob_rows.astype(jnp.bfloat16),
            grad_heads,
            preferred_element_type=jnp.float32,
        )
        return (grad_query, (grad_key_block, grad_value_block))

    start_query = jnp.zeros(query_heads.shape, jnp.float32)
    grad_query, block_grads = lax.scan(
        spread_grads, start_query, (key_blocks, value_blocks, keep_blocks)
    )
    total_rows = key_heads.shape[0]
    model_width = head_count * query_heads.shape[2]
    grad_key_all = block_grads[0].reshape(total_rows, model_width)
    grad_value_all = block_grads[1].reshape(total_rows, model_width)
    return (grad_query * score_scale, grad_key_all, grad_value_all)


def column_sum(matrix_low):
    return jnp.sum(matrix_low.astype(jnp.float32), axis=0)


def body(
    tokens_in,
    lengths,
    ln1_gain,
    ln1_bias,
    w_qkv,
    bias_query,
    bias_value,
    w_out,
    bias_out,
    ln2_gain,
    ln2_bias,
    w_up,
    bias_up,
    w_down,
    bias_down,
    proj_patch,
    proj_class,
    class_emb,
    d_masks,
):
    row_count, model_width = tokens_in.shape
    head_size = HEAD_DIM
    head_count = model_width // head_size
    seq_devices = lax.axis_size("seq")
    grp_devices = lax.axis_size("grp")
    seq_total = row_count * seq_devices
    key_span = min(512, seq_total)
    score_scale = head_size ** (-0.5)
    mask_scale = math.sqrt(model_width)
    length_here = lengths[0]
    first_row = lax.axis_index("seq") * row_count
    valid_rows = (first_row + jnp.arange(row_count, dtype=jnp.int32) < length_here).astype(
        jnp.float32
    )
    key_keep = jnp.arange(seq_total, dtype=jnp.int32) < length_here
    tokens = tokens_in.astype(jnp.float32)
    normed_one, norm_one_back = jax.vjp(layer_norm, tokens, ln1_gain, ln1_bias)
    normed_low = normed_one.astype(jnp.bfloat16)
    zero_keys = jnp.zeros_like(bias_query)
    mixed = jnp.dot(normed_low, w_qkv, preferred_element_type=jnp.float32)
    mixed = mixed + jnp.concatenate([bias_query, zero_keys, bias_value])
    mixed_low = mixed.astype(jnp.bfloat16)
    query_heads = mixed_low[:, :model_width].reshape(row_count, head_count, head_size)
    key_rows = mixed_low[:, model_width : 2 * model_width]
    value_rows = mixed_low[:, 2 * model_width :]
    key_all, value_all = (
        lax.all_gather(key_rows, "seq", axis=0, tiled=True),
        lax.all_gather(value_rows, "seq", axis=0, tiled=True),
    )
    key_heads = key_all.reshape(seq_total, head_count, head_size)
    value_heads = value_all.reshape(seq_total, head_count, head_size)
    attended, log_mass = attend_forward(
        query_heads, key_heads, value_heads, key_keep, score_scale, key_span
    )
    attended_low = attended.reshape(row_count, model_width).astype(jnp.bfloat16)
    branch = jnp.dot(attended_low, w_out, preferred_element_type=jnp.float32) + bias_out
    middle = tokens + branch
    normed_two, norm_two_back = jax.vjp(layer_norm, middle, ln2_gain, ln2_bias)
    normed_two_low = normed_two.astype(jnp.bfloat16)
    hidden = jnp.dot(normed_two_low, w_up, preferred_element_type=jnp.float32) + bias_up
    active, gelu_back = jax.vjp(gelu_exact, hidden)
    active_low = active.astype(jnp.bfloat16)
    final = middle + (jnp.dot(active_low, w_down, preferred_element_type=jnp.float32) + bias_down)
    final_low = final.astype(jnp.bfloat16)
    patches = jnp.dot(final_low, proj_patch, preferred_element_type=jnp.float32)
    patch_unit, patch_back = jax.vjp(unit_rows, patches)
    patch_low = patch_unit.astype(jnp.bfloat16)
    classes = jnp.dot(class_emb, proj_class, preferred_element_type=jnp.float32)
    class_unit, class_back = jax.vjp(unit_rows, classes)
    class_low = class_unit.astype(jnp.bfloat16)
    mask_out = jnp.einsum("rd,cd->rc", patch_low, class_low, preferred_element_type=jnp.float32)
    mask_out = (mask_out * mask_scale * valid_rows[:, None]).astype(jnp.bfloat16)
    mask_grad = (d_masks.astype(jnp.float32) * valid_rows[:, None]).astype(jnp.bfloat16)
    grad_patch_unit = jnp.dot(mask_grad, class_low, preferred_element_type=jnp.float32) * mask_scale
    class_part = (
        jnp.einsum("rc,rd->cd", mask_grad, patch_low, preferred_element_type=jnp.float32)
        * mask_scale
    )
    class_total = lax.psum(class_part, ("grp", "seq"))
    grad_classes = class_back(class_total)[0].astype(jnp.bfloat16)
    class_proj_full = jnp.einsum(
        "cd,ce->de", class_emb, grad_classes, preferred_element_type=jnp.float32
    )
    class_emb_full = jnp.einsum(
        "ce,de->cd", grad_classes, proj_class, preferred_element_type=jnp.float32
    )
    grad_patches = patch_back(grad_patch_unit)[0].astype(jnp.bfloat16)
    grad_proj_patch = jnp.einsum(
        "rd,re->de", final_low, grad_patches, preferred_element_type=jnp.float32
    )
    grad_final = jnp.einsum(
        "re,de->rd", grad_patches, proj_patch, preferred_element_type=jnp.float32
    )
    grad_feed = grad_final.astype(jnp.bfloat16)
    grad_w_down = jnp.einsum("rf,rd->fd", active_low, grad_feed, preferred_element_type=jnp.float32)
    grad_bias_down = column_sum(grad_feed)
    grad_active = jnp.einsum("rd,fd->rf", grad_feed, w_down, preferred_element_type=jnp.float32)
    grad_hidden = gelu_back(grad_active)[0].astype(jnp.bfloat16)
    grad_w_up = jnp.einsum(
        "rd,rf->df", normed_two_low, grad_hidden, preferred_element_type=jnp.float32
    )
    grad_bias_up = column_sum(grad_hidden)
    grad_normed_two = jnp.einsum("rf,df->rd", grad_hidden, w_up, preferred_element_type=jnp.float32)
    grad_middle_norm, grad_ln2_gain, grad_ln2_bias = norm_two_back(grad_normed_two)
    grad_middle = grad_final + grad_middle_norm
    grad_branch = grad_middle.astype(jnp.bfloat16)
    grad_w_out = jnp.einsum(
        "rd,re->de", attended_low, grad_branch, preferred_element_type=jnp.float32
    )
    grad_bias_out = column_sum(grad_branch)
    grad_attended = jnp.einsum("re,de->rd", grad_branch, w_out, preferred_element_type=jnp.float32)
    grad_heads = grad_attended.astype(jnp.bfloat16).reshape(row_count, head_count, head_size)
    grad_query, grad_key_all, grad_value_all = attend_backward(
        query_heads,
        key_heads,
        value_heads,
        key_keep,
        grad_heads,
        log_mass,
        attended,
        score_scale,
        key_span,
    )
    grad_key_own, grad_value_own = (
        lax.psum_scatter(
            grad_key_all.astype(jnp.bfloat16), "seq", scatter_dimension=0, tiled=True
        ).astype(jnp.float32),
        lax.psum_scatter(
            grad_value_all.astype(jnp.bfloat16), "seq", scatter_dimension=0, tiled=True
        ).astype(jnp.float32),
    )
    grad_mixed = jnp.concatenate(
        [grad_query.reshape(row_count, model_width), grad_key_own, grad_value_own], axis=1
    ).astype(jnp.bfloat16)
    grad_w_qkv = jnp.einsum("rd,rm->dm", normed_low, grad_mixed, preferred_element_type=jnp.float32)
    grad_bias_all = column_sum(grad_mixed)
    grad_bias_query = grad_bias_all[:model_width]
    grad_bias_value = grad_bias_all[2 * model_width :]
    grad_normed_one = jnp.einsum("rm,dm->rd", grad_mixed, w_qkv, preferred_element_type=jnp.float32)
    grad_tokens_norm, grad_ln1_gain, grad_ln1_bias = norm_one_back(grad_normed_one)
    grad_tokens = (grad_middle + grad_tokens_norm).astype(jnp.bfloat16)
    row_parts = (
        lax.psum_scatter(grad_w_qkv, "grp", scatter_dimension=0, tiled=True),
        lax.psum_scatter(grad_w_out, "grp", scatter_dimension=0, tiled=True),
        lax.psum_scatter(grad_w_up, "grp", scatter_dimension=0, tiled=True),
        lax.psum_scatter(grad_w_down, "grp", scatter_dimension=0, tiled=True),
        lax.psum_scatter(grad_proj_patch, "grp", scatter_dimension=0, tiled=True),
        lax.psum_scatter(grad_ln1_gain, "grp", scatter_dimension=0, tiled=True),
        lax.psum_scatter(grad_ln1_bias, "grp", scatter_dimension=0, tiled=True),
        lax.psum_scatter(grad_bias_query, "grp", scatter_dimension=0, tiled=True),
        lax.psum_scatter(grad_bias_value, "grp", scatter_dimension=0, tiled=True),
        lax.psum_scatter(grad_bias_out, "grp", scatter_dimension=0, tiled=True),
        lax.psum_scatter(grad_ln2_gain, "grp", scatter_dimension=0, tiled=True),
        lax.psum_scatter(grad_ln2_bias, "grp", scatter_dimension=0, tiled=True),
        lax.psum_scatter(grad_bias_up, "grp", scatter_dimension=0, tiled=True),
        lax.psum_scatter(grad_bias_down, "grp", scatter_dimension=0, tiled=True),
    )
    matrix_parts = (
        lax.psum_scatter(
            row_parts[0].astype(jnp.bfloat16), "seq", scatter_dimension=1, tiled=True
        ).astype(jnp.float32),
        lax.psum_scatter(
            row_parts[1].astype(jnp.bfloat16), "seq", scatter_dimension=1, tiled=True
        ).astype(jnp.float32),
        lax.psum_scatter(
            row_parts[2].astype(jnp.bfloat16), "seq", scatter_dimension=1, tiled=True
        ).astype(jnp.float32),
        lax.psum_scatter(
            row_parts[3].astype(jnp.bfloat16), "seq", scatter_dimension=1, tiled=True
        ).astype(jnp.float32),
        lax.psum_scatter(
            row_parts[4].astype(jnp.bfloat16), "seq", scatter_dimension=1, tiled=True
        ).astype(jnp.float32),
    )
    vector_parts = lax.psum(
        (
            row_parts[5],
            row_parts[6],
            row_parts[7],
            row_parts[8],
            row_parts[9],
            row_parts[10],
            row_parts[11],
            row_parts[12],
            row_parts[13],
        ),
        "seq",
    )
    rows_each = model_width // grp_devices
    cols_each = model_width // seq_devices
    grp_here = lax.axis_index("grp")
    seq_here = lax.axis_index("seq")
    grad_proj_class = lax.dynamic_slice(
        class_proj_full, (grp_here * rows_each, seq_here * cols_each), (rows_each, cols_each)
    )
    grad_class_emb = lax.dynamic_slice_in_dim(class_emb_full, grp_here * rows_each, rows_each, 1)
    return (
        mask_out,
        grad_tokens,
        vector_parts[0],
        vector_parts[1],
        matrix_parts[0],
        vector_parts[2],
        vector_parts[3],
        matrix_parts[1],
        vector_parts[4],
        vector_parts[5],
        vector_parts[6],
        matrix_parts[2],
        vector_parts[7],
        matrix_parts[3],
        vector_parts[8],
        matrix_parts[4],
        grad_proj_class,
        grad_class_emb,
    )


def solution(mesh):
    return jax.shard_map(
        body,
        mesh=mesh,
        in_specs=(
            P(("grp", "seq"), None),
            P("grp"),
            P(),
            P(),
            P(),
            P(),
            P(),
            P(),
            P(),
            P(),
            P(),
            P(),
            P(),
            P(),
            P(),
            P(),
            P(),
            P(),
            P(("grp", "seq"), None),
        ),
        out_specs=(
            P(("grp", "seq"), None),
            P(("grp", "seq"), None),
            P("grp"),
            P("grp"),
            P("grp", "seq"),
            P("grp"),
            P("grp"),
            P("grp", "seq"),
            P("grp"),
            P("grp"),
            P("grp"),
            P("grp", "seq"),
            P("grp"),
            P("grp", "seq"),
            P("grp"),
            P("grp", "seq"),
            P("grp", "seq"),
            P(None, "grp"),
        ),
        check_vma=False,
    )
```

profile of v0, /device:TPU:0, one launch (start us, length us, event | category | flops | bytes accessed | tf_op | source)
XLA Modules:
  0.0 1562.4 jit_solution(7666178320111044407)
XLA Ops:
  30.2 29.2 %all-gather.5.cloned.1.call-done = bf16[3072,768]{1,0:T(8,128)(2,1)} async-done(((bf16[768,768]{1,0:T(8,128)(2,1)}), bf16[3072,768]{1,0:T(8,128)(2,1)}) %all-gather.5.cloned.1.call-update) | async-done | bytes 4718608 | tf_op jit(solution)/shard_map/all_gather | solution.py:183
  59.4 15.0 reshape.189
  74.4 13.5 copy.80
  88.0 165.2 %while.39 = (s32[]{:T(128)}, f32[12,768]{1,0:T(8,128)}, f32[12,768]{1,0:T(8,128)}, pred[6,512]{1,0:T(8,128)(4,1)S(1)}, bf16[6,512,12,64]{1,3,2,0:T(8,128)(2,1)},...) while((s32[]{:T(128)}, f32[12,768]{1,0:T(8,128)}, f32[12,768]{1,0:T(8,128)}, ...), condition=%wide.region_5.6_spmd.clone, body=%wide.region_2.5_spmd.clone.sunk | while | flops 637056000 | bytes 40196704 | solution.py:65
  88.0 12.4 bitcast_reduce_fusion.2
  115.5 12.3 bitcast_reduce_fusion.2
  143.0 12.3 bitcast_reduce_fusion.2
  170.6 12.3 bitcast_reduce_fusion.2
  198.1 12.3 bitcast_reduce_fusion.2
  211.9 10.8 fusion.145
  225.6 12.3 bitcast_reduce_fusion.2
  253.2 15.0 reshape.188
  268.1 13.6 copy.79
  283.2 61.1 %while.40 = (s32[]{:T(128)}, f32[768,12,64]{0,2,1:T(8,128)}, bf16[6,512,12,64]{1,3,2,0:T(8,128)(2,1)}, pred[6,512]{1,0:T(8,128)(4,1)S(1)}, bf16[6,512,12,64]{1,3...) while((s32[]{:T(128)}, f32[768,12,64]{0,2,1:T(8,128)}, ...), condition=%wide.region_7.8_spmd.clone, body=%wide.region_6.7_spmd.clone.sunk | while | flops 1228013568 | bytes 7522923 | solution.py:78
  350.3 28.6 %multiply_convert_fusion.1 = (bf16[768,3072]{1,0:T(8,128)(2,1)S(1)}, f32[768,3072]{1,0:T(8,128)}, f32[768,3072]{1,0:T(8,128)}) fusion(f32[3072]{0:T(1024)S(1)} %copy-done.54, bf16[768,3072]{1,0:T(8,128)(2,1)S(1)} %bitcast.171, f32[768,768]{0,1:T(8,128)S(1)} %get-tuple-element.449, f32[768]{0:T(1024)S(1)} %copy-done.57, f32[768]{0:T(1024)S(1)} %copy-done.42, ...), kind=kOutput, calls=%fused_computation.51 | convolution fusion | flops 3782541312 | bytes 30695424 | tf_op jit(solution)/shard_map/dot_general | solution.py:196
  395.1 13.0 convert_reduce_fusion
  433.9 291.4 %while.41 = (s32[]{:T(128)}, f32[768,12,64]{0,2,1:T(8,128)}, bf16[6,512,12,64]{1,3,2,0:T(8,128)(2,1)}, bf16[6,512,12,64]{1,3,2,0:T(8,128)(2,1)}, bf16[6,512,12,6...) while((s32[]{:T(128)}, f32[768,12,64]{0,2,1:T(8,128)}, ...), condition=%wide.region_16.17_spmd.clone, body=%wide.region_15.16_spmd.clone.sunk | while | flops 3068657664 | bytes 142766832 | solution.py:122
  445.0 10.9 multiply_convert_fusion.13
  470.6 11.9 bitcast_dynamic-update-slice_fusion.5
  493.2 10.8 multiply_convert_fusion.13
  519.2 11.9 bitcast_dynamic-update-slice_fusion.5
  567.8 11.9 bitcast_dynamic-update-slice_fusion.5
  616.3 11.9 bitcast_dynamic-update-slice_fusion.5
  664.8 11.9 bitcast_dynamic-update-slice_fusion.5
  713.3 11.8 bitcast_dynamic-update-slice_fusion.5
  784.4 50.4 %reduce-scatter.23.cloned.1.call-done = bf16[768,768]{0,1:T(8,128)(2,1)} async-done(((bf16[3072,768]{0,1:T(8,128)(2,1)}), bf16[768,768]{0,1:T(8,128)(2,1)}) %reduce-scatter.23.cloned.1.call-update) | async-done | bytes 1179664 | tf_op jit(solution)/shard_map/reduce_scatter | solution.py:264
  848.8 118.0 %all-reduce.13.cloned.1.call-done = f32[150,768]{1,0:T(8,128)} async-done(((f32[150,768]{1,0:T(8,128)}), f32[150,768]{1,0:T(8,128)}) %all-reduce.13.cloned.1.call-update) | async-done | bytes 460816 | tf_op jit(solution)/shard_map/psum | solution.py:215
  968.6 165.9 %reduce-scatter.33.cloned.1.call-done = f32[384,768]{1,0:T(8,128)} async-done(((f32[3072,768]{1,0:T(8,128)}), f32[384,768]{1,0:T(8,128)}) %reduce-scatter.33.cloned.1.call-update) | async-done | bytes 1179664 | tf_op jit(solution)/shard_map/reduce_scatter | solution.py:282
  1159.6 19.8 %reduce-scatter.39.cloned.1.call-done = bf16[192,96]{1,0:T(8,128)(2,1)} async-done(((bf16[768,96]{1,0:T(8,128)(2,1)}), bf16[192,96]{1,0:T(8,128)(2,1)}) %reduce-scatter.39.cloned.1.call-update) | async-done | bytes 36880
  1182.3 164.4 %reduce-scatter.29.cloned.1.call-done = f32[96,3072]{1,0:T(8,128)} async-done(((f32[768,3072]{1,0:T(8,128)}), f32[96,3072]{1,0:T(8,128)}) %reduce-scatter.29.cloned.1.call-update) | async-done | bytes 1179664 | tf_op jit(solution)/shard_map/reduce_scatter | solution.py:281
  1366.1 112.8 %reduce-scatter.25.cloned.1.call-done = f32[96,2304]{1,0:T(8,128)} async-done(((f32[768,2304]{1,0:T(8,128)}), f32[96,2304]{1,0:T(8,128)}) %reduce-scatter.25.cloned.1.call-update) | async-done | bytes 884752 | tf_op jit(solution)/shard_map/reduce_scatter | solution.py:279
  1484.3 36.8 %all-reduce.9 = (f32[768]{0:T(1024)}, f32[768]{0:T(1024)}, f32[768]{0:T(1024)}, f32[768]{0:T(1024)}, f32[768]{0:T(1024)}, /*index=5*/f32[768]{0:T(1024)}, f32[768]{0:T(1024)}, f32[3072]{0:T(1024)}, f32[768]{0:T(1024)}) all-reduce(f32[768]{0:T(1024)} %get-tuple-element.362, ...), channel_id=4, replica_groups=mesh['grp'=8,'seq'=4] {'grp'}, use_global_device_ids=true, to_apply=%region_22.23.clone | all-reduce | flops 9216 | bytes 73728
  (381 shorter events, 570.3 us)
Async XLA Ops:
  7.2 52.1 %all-gather.5.cloned.1.call-start = ((), (), s32[]{:S(2)}) async-start(), calls=%async_computation.13 | async-start | bytes 5898240 | tf_op jit(solution)/shard_map/all_gather | solution.py:183
  19.1 234.1 %all-gather.3.cloned.1.call-start = ((), (), s32[]{:S(2)}) async-start(), calls=%async_computation.12 | async-start | bytes 5898240 | tf_op jit(solution)/shard_map/all_gather | solution.py:184
  19.8 742.3 %reduce-scatter.35.cloned.1.call-start = ((), (), s32[]{:S(2)}) async-start(), calls=%async_computation.21 | async-start | bytes 2654208 | tf_op jit(solution)/shard_map/reduce_scatter | solution.py:283
  26.3 48.1 %copy-start.40 = (f32[150]{0:T(256)}, f32[150]{0:T(256)S(1)}, u32[]{:S(2)}) copy-start(f32[150]{0:T(256)S(1)} %add_rsqrt_fusion.1) | copy-start | bytes 1804
  346.6 32.3 %slice-start = ((s8[4718592]{0:T(1024)(128)(4,1)}), s8[4194304]{0:T(1024)(128)(4,1)S(1)}, s32[]{:S(2)}) async-start(s8[4718592]{0:T(1024)(128)(4,1)} %bitcast.168), calls=%async_computation.27 | async-start | bytes 8388608
  347.9 31.0 %copy-start.7 = (f32[768,768]{0,1:T(8,128)}, f32[768,768]{0,1:T(8,128)S(1)}, u32[]{:S(2)}) copy-start(f32[768,768]{0,1:T(8,128)S(1)} %get-tuple-element.449) | copy-start | bytes 7077892
  348.0 77.0 %copy-start.24 = (f32[768]{0:T(1024)}, f32[768]{0:T(1024)S(1)}, u32[]{:S(2)}) copy-start(f32[768]{0:T(1024)S(1)} %broadcast_multiply_fusion.1) | copy-start | bytes 9220
  350.3 74.7 %copy-start.38 = (f32[768]{0:T(1024)}, f32[768]{0:T(1024)S(1)}, u32[]{:S(2)}) copy-start(f32[768]{0:T(1024)S(1)} %fusion.66) | copy-start | bytes 9220
  350.3 28.7 %slice-start.1 = ((s8[4718592]{0:T(1024)(128)(4,1)}), s8[524288]{0:T(1024)(128)(4,1)S(1)}, s32[]{:S(2)}) async-start(s8[4718592]{0:T(1024)(128)(4,1)} %bitcast.168), calls=%async_computation.28 | async-start | bytes 1048576
  350.3 28.7 %copy-start.56 = (f32[768]{0:T(1024)S(1)}, f32[768]{0:T(1024)}, u32[]{:S(2)}) copy-start(f32[768]{0:T(1024)} %param.39) | copy-start | bytes 9220
  391.7 373.9 %reduce-scatter.27.cloned.1.call-start = ((), (), s32[]{:S(2)}) async-start(), calls=%async_computation.17 | async-start | bytes 2654208 | tf_op jit(solution)/shard_map/reduce_scatter | solution.py:280
  433.8 350.6 %reduce-scatter.21.cloned.1.call-start = ((), (), s32[]{:S(2)}) async-start(), calls=%async_computation.14 | async-start | bytes 5898240 | tf_op jit(solution)/shard_map/reduce_scatter | solution.py:261
  445.0 14.6 copy-start.2
  493.2 14.5 copy-start.2
  541.8 14.4 copy-start.2
  590.4 14.4 copy-start.2
  638.8 14.4 copy-start.2
  687.3 14.4 copy-start.2
  736.2 98.6 %reduce-scatter.23.cloned.1.call-start = ((), (), s32[]{:S(2)}) async-start(), calls=%async_computation.15 | async-start | bytes 5898240 | tf_op jit(solution)/shard_map/reduce_scatter | solution.py:264
  747.4 219.4 %all-reduce.13.cloned.1.call-start = ((), (), s32[]{:S(2)}) async-start(), calls=%async_computation.22 | async-start | bytes 933888 | tf_op jit(solution)/shard_map/psum | solution.py:215
  751.3 383.3 %reduce-scatter.33.cloned.1.call-start = ((), (), s32[]{:S(2)}) async-start(), calls=%async_computation.20 | async-start | bytes 10616832 | tf_op jit(solution)/shard_map/reduce_scatter | solution.py:282
  762.0 394.6 %reduce-scatter.43.cloned.1.call-start = ((), (), s32[]{:S(2)}) async-start(), calls=%async_computation.26 | async-start | bytes 245760
  765.5 413.9 %reduce-scatter.39.cloned.1.call-start = ((), (), s32[]{:S(2)}) async-start(), calls=%async_computation.24 | async-start | bytes 245760
  769.0 577.8 %reduce-scatter.29.cloned.1.call-start = ((), (), s32[]{:S(2)}) async-start(), calls=%async_computation.18 | async-start | bytes 10616832 | tf_op jit(solution)/shard_map/reduce_scatter | solution.py:281
  780.0 54.9 %copy-start.23 = (f32[768]{0:T(1024)S(1)}, f32[768]{0:T(1024)}, u32[]{:S(2)}) copy-start(f32[768]{0:T(1024)} %copy-done.22) | copy-start | bytes 9220
  780.0 54.9 %copy-start.32 = (f32[768]{0:T(1024)S(1)}, f32[768]{0:T(1024)}, u32[]{:S(2)}) copy-start(f32[768]{0:T(1024)} %copy-done.31) | copy-start | bytes 9220
  780.0 54.9 %copy-start.36 = (f32[768]{0:T(1024)S(1)}, f32[768]{0:T(1024)}, u32[]{:S(2)}) copy-start(f32[768]{0:T(1024)} %param.27) | copy-start | bytes 9220
  780.0 698.9 %reduce-scatter.25.cloned.1.call-start = ((), (), s32[]{:S(2)}) async-start(), calls=%async_computation.16 | async-start | bytes 7962624 | tf_op jit(solution)/shard_map/reduce_scatter | solution.py:279
  843.3 703.7 %reduce-scatter.41.cloned.1.call-start = ((), (), s32[]{:S(2)}) async-start(), calls=%async_computation.25 | async-start | bytes 737280
  848.8 290.8 %copy-start.41 = (f32[150]{0:T(256)S(1)}, f32[150]{0:T(256)}, u32[]{:S(2)}) copy-start(f32[150]{0:T(256)} %copy-done.40) | copy-start | bytes 1804
  1138.9 411.6 %reduce-scatter.31.cloned.1.call-start = ((), (), s32[]{:S(2)}) async-start(), calls=%async_computation.19 | async-start | bytes 737280 | tf_op jit(solution)/shard_map/reduce_scatter | solution.py:301
  1348.9 203.2 %reduce-scatter.37.cloned.1.call-start = ((), (), s32[]{:S(2)}) async-start(), calls=%async_computation.23 | async-start | bytes 737280
  (68 other events, 315.5 us)
Sparse Core Ops, SparseCore 0:
  19.2 40.1 all-gather.4
  60.9 37.4 all-gather.2
  391.8 69.1 reduce-scatter.34
  464.4 68.0 reduce-scatter.26
  736.4 48.0 reduce-scatter.20
  787.0 47.8 reduce-scatter.22
  840.2 126.5 all-reduce.12
  970.8 163.7 reduce-scatter.32
  1137.7 18.8 reduce-scatter.42
  1159.6 19.7 reduce-scatter.38
  1183.4 163.2 reduce-scatter.28
  1350.7 128.1 reduce-scatter.24
  1481.4 21.1 reduce-scatter.40
  1504.9 22.0 reduce-scatter.30
  1529.4 22.0 reduce-scatter.36
where the time goes:
time: 1570 us; the launch traced here: 1560 us
  waiting for transfers between devices  671 us (43%)
  matrix products  526 us (34%)
  local copies, waits for them, and re-layouts  171 us (11%)
  other arithmetic  131 us (8%)
  blocking collectives  43.3 us (3%)
  between operations  17.1 us (1%)
    reduce_scatter x1, waiting for transfers between devices, body(): lax.psum_scatter(grad_w_down, 'grp', scatter_dimension=0, tiled=True)  166 us
    reduce_scatter x1, waiting for transfers between devices, body(): lax.psum_scatter(grad_w_up, 'grp', scatter_dimension=0, tiled=True)  164 us
    dot_general x12, matrix products, score_block(): jnp.einsum('qhd,khd->hqk', query_heads, key_block, preferred_element_type...  138 us
    psum x1, waiting for transfers between devices, body(): class_total = lax.psum(class_part, ('grp', 'seq'))  118 us
    reduce_scatter x1, waiting for transfers between devices, body(): lax.psum_scatter(grad_w_qkv, 'grp', scatter_dimension=0, tiled=True)  113 us
    unnamed x148, local copies, waits for them, and re-layouts  81.5 us
    dot_general x6, matrix products, spread_grads(): jnp.einsum('hqk,qhd->khd', prob_rows.astype(jnp.bfloat16), grad_heads, pr...  71.3 us
    reduce_sum x6, other arithmetic, gather_stats(): jnp.sum(jnp.exp(scores - new_top[..., None]), axis=-1)  64.9 us
  transfers between devices with their start and end apart: 15, of which 9 were waited for; matrix products, arithmetic and copies ran while one was open for 41% of the time, Pallas kernels for 0%

commit v1 on v0

--- a/solution.py
+++ b/solution.py
@@ -212,7 +212,12 @@
         jnp.einsum("rc,rd->cd", mask_grad, patch_low, preferred_element_type=jnp.float32)
         * mask_scale
     )
-    class_total = lax.psum(class_part, ("grp", "seq"))
+
+    def turn_rings_now(target, row_axis):
+        formed = jnp.sum(jax.lax.all_gather(target, row_axis), 0)
+        return formed
+
+    class_total = turn_rings_now(class_part, row_axis=("grp", "seq"))
     grad_classes = class_back(class_total)[0].astype(jnp.bfloat16)
     class_proj_full = jnp.einsum(
         "cd,ce->de", class_emb, grad_classes, preferred_element_type=jnp.float32

time: 1570 us -> 1700 us (1.083)
  waiting for transfers between devices: 671 us -> 791 us
    psum x1 -> x0, waiting for transfers between devices: 118 us -> none  [body(): class_total = lax.psum(class_part, ('grp', 'seq'))]
    all_gather x0 -> x1, waiting for transfers between devices: none -> 92.5 us  [turn_rings_now(): formed = jnp.sum(jax.lax.all_gather(target, row_axis), 0)]
    reduce_scatter x1, waiting for transfers between devices: 0.02 us -> 68 us  [body(): lax.psum_scatter(grad_w_out, 'grp', scatter_dimension=0, tiled=True)]
    reduce_scatter x1, waiting for transfers between devices: 0.02 us -> 64.1 us  [body(): lax.psum_scatter(grad_proj_patch, 'grp', scatter_dimension=0, tiled=True)]
    unnamed x148 -> x156, local copies, waits for them, and re-layouts: 81.5 us -> 80 us
  transfers between devices with their start and end apart: 15 -> 15, of which waited for: 9 -> 11; matrix products, arithmetic and copies ran while one was open for 41% -> 19% of each run, Pallas kernels for 0% -> 0%
where the time goes in v1:
time: 1700 us; the launch traced here: 1690 us
  waiting for transfers between devices  791 us (47%)
  matrix products  528 us (31%)
  local copies, waits for them, and re-layouts  169 us (10%)
  other arithmetic  136 us (8%)
  blocking collectives  45.2 us (3%)
  between operations  17 us (1%)
    reduce_scatter x1, waiting for transfers between devices, body(): lax.psum_scatter(grad_w_down, 'grp', scatter_dimension=0, tiled=True)  163 us
    reduce_scatter x1, waiting for transfers between devices, body(): lax.psum_scatter(grad_w_up, 'grp', scatter_dimension=0, tiled=True)  162 us
    dot_general x12, matrix products, score_block(): jnp.einsum('qhd,khd->hqk', query_heads, key_block, preferred_element_type...  138 us
    reduce_scatter x1, waiting for transfers between devices, body(): lax.psum_scatter(grad_w_qkv, 'grp', scatter_dimension=0, tiled=True)  130 us
    all_gather x1, waiting for transfers between devices, turn_rings_now(): formed = jnp.sum(jax.lax.all_gather(target, row_axis), 0)  92.5 us
    unnamed x156, local copies, waits for them, and re-layouts  80 us
    dot_general x6, matrix products, spread_grads(): jnp.einsum('hqk,qhd->khd', prob_rows.astype(jnp.bfloat16), grad_heads, pr...  71.2 us
    reduce_scatter x1, waiting for transfers between devices, body(): lax.psum_scatter(grad_w_out, 'grp', scatter_dimension=0, tiled=True)  68 us
  transfers between devices with their start and end apart: 15, of which 11 were waited for; matrix products, arithmetic and copies ran while one was open for 19% of the time, Pallas kernels for 0%

profile of v1, /device:TPU:0, one launch (start us, length us, event | category | flops | bytes accessed | tf_op | source)
XLA Modules:
  0.0 1688.4 jit_solution(727994105951766784)
XLA Ops:
  30.1 29.3 %all-gather.8.cloned.1.call-done = bf16[3072,768]{1,0:T(8,128)(2,1)} async-done(((bf16[768,768]{1,0:T(8,128)(2,1)}), bf16[3072,768]{1,0:T(8,128)(2,1)}) %all-gather.8.cloned.1.call-update) | async-done | bytes 4718608 | tf_op jit(solution)/shard_map/all_gather | solution.py:183
  59.4 15.1 reshape.193
  74.4 13.5 copy.80
  88.0 165.2 %while.39 = (s32[]{:T(128)}, f32[12,768]{1,0:T(8,128)}, f32[12,768]{1,0:T(8,128)}, pred[6,512]{1,0:T(8,128)(4,1)S(1)}, bf16[6,512,12,64]{1,3,2,0:T(8,128)(2,1)},...) while((s32[]{:T(128)}, f32[12,768]{1,0:T(8,128)}, f32[12,768]{1,0:T(8,128)}, ...), condition=%wide.region_5.6_spmd.clone, body=%wide.region_2.5_spmd.clone.sunk | while | flops 637056000 | bytes 40196704 | solution.py:65
  88.0 12.3 bitcast_reduce_fusion.2
  101.8 10.8 fusion.146
  115.5 12.3 bitcast_reduce_fusion.2
  143.0 12.3 bitcast_reduce_fusion.2
  170.6 12.3 bitcast_reduce_fusion.2
  198.1 12.3 bitcast_reduce_fusion.2
  225.7 12.3 bitcast_reduce_fusion.2
  253.2 15.0 reshape.192
  268.2 13.6 copy.79
  283.2 61.5 %while.40 = (s32[]{:T(128)}, f32[768,12,64]{0,2,1:T(8,128)}, bf16[6,512,12,64]{1,3,2,0:T(8,128)(2,1)}, pred[6,512]{1,0:T(8,128)(4,1)S(1)}, bf16[6,512,12,64]{1,3...) while((s32[]{:T(128)}, f32[768,12,64]{0,2,1:T(8,128)}, ...), condition=%wide.region_7.8_spmd.clone, body=%wide.region_6.7_spmd.clone.sunk | while | flops 1228013568 | bytes 7522923 | solution.py:78
  350.7 28.6 %multiply_convert_fusion.1 = (bf16[768,3072]{1,0:T(8,128)(2,1)S(1)}, f32[768,3072]{1,0:T(8,128)}, f32[768,3072]{1,0:T(8,128)}) fusion(f32[3072]{0:T(1024)S(1)} %copy-done.55, bf16[768,3072]{1,0:T(8,128)(2,1)S(1)} %bitcast.173, f32[768,768]{0,1:T(8,128)S(1)} %get-tuple-element.449, f32[768]{0:T(1024)S(1)} %copy-done.58, f32[768]{0:T(1024)S(1)} %copy-done.42, ...), kind=kOutput, calls=%fused_computation.51 | convolution fusion | flops 3782541312 | bytes 30695424 | tf_op jit(solution)/shard_map/dot_general | solution.py:196
  392.7 12.7 convert_reduce_fusion
  428.1 290.7 %while.41 = (s32[]{:T(128)}, f32[768,12,64]{0,2,1:T(8,128)}, bf16[6,512,12,64]{1,3,2,0:T(8,128)(2,1)}, bf16[6,512,12,64]{1,3,2,0:T(8,128)(2,1)}, bf16[6,512,12,6...) while((s32[]{:T(128)}, f32[768,12,64]{0,2,1:T(8,128)}, ...), condition=%wide.region_16.17_spmd.clone, body=%wide.region_15.16_spmd.clone.sunk | while | flops 3068657664 | bytes 142766832 | solution.py:122
  464.3 11.9 bitcast_dynamic-update-slice_fusion.5
  512.7 11.9 bitcast_dynamic-update-slice_fusion.5
  561.2 11.9 bitcast_dynamic-update-slice_fusion.5
  609.6 11.9 bitcast_dynamic-update-slice_fusion.5
  658.1 11.9 bitcast_dynamic-update-slice_fusion.5
  706.6 11.8 bitcast_dynamic-update-slice_fusion.5
  778.0 50.4 %reduce-scatter.23.cloned.1.call-done = bf16[768,768]{0,1:T(8,128)(2,1)} async-done(((bf16[3072,768]{0,1:T(8,128)(2,1)}), bf16[768,768]{0,1:T(8,128)(2,1)}) %reduce-scatter.23.cloned.1.call-update) | async-done | bytes 1179664 | tf_op jit(solution)/shard_map/reduce_scatter | solution.py:269
  836.9 64.1 %reduce-scatter.35.cloned.1.call-done = f32[96,768]{1,0:T(8,128)} async-done(((f32[768,768]{1,0:T(8,128)}), f32[96,768]{1,0:T(8,128)}) %reduce-scatter.35.cloned.1.call-update) | async-done | bytes 294928 | tf_op jit(solution)/shard_map/reduce_scatter | solution.py:288
  904.4 68.0 %reduce-scatter.27.cloned.1.call-done = f32[96,768]{1,0:T(8,128)} async-done(((f32[768,768]{1,0:T(8,128)}), f32[96,768]{1,0:T(8,128)}) %reduce-scatter.27.cloned.1.call-update) | async-done | bytes 294928 | tf_op jit(solution)/shard_map/reduce_scatter | solution.py:285
  975.9 162.7 %reduce-scatter.33.cloned.1.call-done = f32[384,768]{1,0:T(8,128)} async-done(((f32[3072,768]{1,0:T(8,128)}), f32[384,768]{1,0:T(8,128)}) %reduce-scatter.33.cloned.1.call-update) | async-done | bytes 1179664 | tf_op jit(solution)/shard_map/reduce_scatter | solution.py:287
  1143.1 161.7 %reduce-scatter.29.cloned.1.call-done = f32[96,3072]{1,0:T(8,128)} async-done(((f32[768,3072]{1,0:T(8,128)}), f32[96,3072]{1,0:T(8,128)}) %reduce-scatter.29.cloned.1.call-update) | async-done | bytes 1179664 | tf_op jit(solution)/shard_map/reduce_scatter | solution.py:286
  1307.1 129.6 %reduce-scatter.25.cloned.1.call-done = f32[96,2304]{1,0:T(8,128)} async-done(((f32[768,2304]{1,0:T(8,128)}), f32[96,2304]{1,0:T(8,128)}) %reduce-scatter.25.cloned.1.call-update) | async-done | bytes 884752 | tf_op jit(solution)/shard_map/reduce_scatter | solution.py:284
  1461.4 19.9 %reduce-scatter.39.cloned.1.call-done = bf16[192,96]{1,0:T(8,128)(2,1)} async-done(((bf16[768,96]{1,0:T(8,128)(2,1)}), bf16[192,96]{1,0:T(8,128)(2,1)}) %reduce-scatter.39.cloned.1.call-update) | async-done | bytes 36880
  1499.6 38.7 %all-reduce.9 = (f32[768]{0:T(1024)}, f32[768]{0:T(1024)}, f32[768]{0:T(1024)}, f32[768]{0:T(1024)}, f32[768]{0:T(1024)}, /*index=5*/f32[768]{0:T(1024)}, f32[768]{0:T(1024)}, f32[3072]{0:T(1024)}, f32[768]{0:T(1024)}) all-reduce(f32[768]{0:T(1024)} %get-tuple-element.362, ...), channel_id=5, replica_groups=mesh['grp'=8,'seq'=4] {'grp'}, use_global_device_ids=true, to_apply=%region_22.23.clone | all-reduce | flops 9216 | bytes 73728
  1572.6 92.5 %all-gather.10.cloned.1.call-done = f32[32,150,768]{2,1,0:T(8,128)} async-done(((f32[1,150,768]{2,1,0:T(8,128)}), f32[32,150,768]{2,1,0:T(8,128)}) %all-gather.10.cloned.1.call-update) | async-done | bytes 14745616 | tf_op jit(solution)/shard_map/all_gather | solution.py:217
  (390 shorter events, 598.8 us)
Async XLA Ops:
  7.2 52.1 %all-gather.8.cloned.1.call-start = ((), (), s32[]{:S(2)}) async-start(), calls=%async_computation.13 | async-start | bytes 5898240 | tf_op jit(solution)/shard_map/all_gather | solution.py:183
  19.1 234.1 %all-gather.6.cloned.1.call-start = ((), (), s32[]{:S(2)}) async-start(), calls=%async_computation.12 | async-start | bytes 5898240 | tf_op jit(solution)/shard_map/all_gather | solution.py:184
  19.8 758.2 %reduce-scatter.21.cloned.1.call-start = ((), (), s32[]{:S(2)}) async-start(), calls=%async_computation.14 | async-start | bytes 5898240 | tf_op jit(solution)/shard_map/reduce_scatter | solution.py:266
  26.3 48.2 %copy-start.40 = (f32[150]{0:T(256)}, f32[150]{0:T(256)S(1)}, u32[]{:S(2)}) copy-start(f32[150]{0:T(256)S(1)} %add_rsqrt_fusion.1) | copy-start | bytes 1804
  347.0 32.3 %slice-start = ((s8[4718592]{0:T(1024)(128)(4,1)}), s8[4194304]{0:T(1024)(128)(4,1)S(1)}, s32[]{:S(2)}) async-start(s8[4718592]{0:T(1024)(128)(4,1)} %bitcast.170), calls=%async_computation.27 | async-start | bytes 8388608
  348.3 31.0 %copy-start.7 = (f32[768,768]{0,1:T(8,128)}, f32[768,768]{0,1:T(8,128)S(1)}, u32[]{:S(2)}) copy-start(f32[768,768]{0,1:T(8,128)S(1)} %get-tuple-element.449) | copy-start | bytes 7077892
  348.3 73.9 %copy-start.22 = (f32[768]{0:T(1024)}, f32[768]{0:T(1024)S(1)}, u32[]{:S(2)}) copy-start(f32[768]{0:T(1024)S(1)} %broadcast_multiply_fusion.1) | copy-start | bytes 9220
  350.7 71.6 %copy-start.38 = (f32[768]{0:T(1024)}, f32[768]{0:T(1024)S(1)}, u32[]{:S(2)}) copy-start(f32[768]{0:T(1024)S(1)} %fusion.67) | copy-start | bytes 9220
  350.7 28.7 %slice-start.1 = ((s8[4718592]{0:T(1024)(128)(4,1)}), s8[524288]{0:T(1024)(128)(4,1)S(1)}, s32[]{:S(2)}) async-start(s8[4718592]{0:T(1024)(128)(4,1)} %bitcast.170), calls=%async_computation.28 | async-start | bytes 1048576
  350.7 28.7 %copy-start.57 = (f32[768]{0:T(1024)S(1)}, f32[768]{0:T(1024)}, u32[]{:S(2)}) copy-start(f32[768]{0:T(1024)} %param.39) | copy-start | bytes 9220
  632.2 14.4 copy-start.2
  730.0 98.5 %reduce-scatter.23.cloned.1.call-start = ((), (), s32[]{:S(2)}) async-start(), calls=%async_computation.15 | async-start | bytes 5898240 | tf_op jit(solution)/shard_map/reduce_scatter | solution.py:269
  741.3 159.7 %reduce-scatter.35.cloned.1.call-start = ((), (), s32[]{:S(2)}) async-start(), calls=%async_computation.21 | async-start | bytes 2654208 | tf_op jit(solution)/shard_map/reduce_scatter | solution.py:288
  745.6 226.9 %reduce-scatter.27.cloned.1.call-start = ((), (), s32[]{:S(2)}) async-start(), calls=%async_computation.17 | async-start | bytes 2654208 | tf_op jit(solution)/shard_map/reduce_scatter | solution.py:285
  749.9 388.7 %reduce-scatter.33.cloned.1.call-start = ((), (), s32[]{:S(2)}) async-start(), calls=%async_computation.20 | async-start | bytes 10616832 | tf_op jit(solution)/shard_map/reduce_scatter | solution.py:287
  760.9 544.0 %reduce-scatter.29.cloned.1.call-start = ((), (), s32[]{:S(2)}) async-start(), calls=%async_computation.18 | async-start | bytes 10616832 | tf_op jit(solution)/shard_map/reduce_scatter | solution.py:286
  772.2 56.2 %copy-start.21 = (f32[768]{0:T(1024)S(1)}, f32[768]{0:T(1024)}, u32[]{:S(2)}) copy-start(f32[768]{0:T(1024)} %copy-done.20) | copy-start | bytes 9220
  772.2 56.2 %copy-start.30 = (f32[768]{0:T(1024)S(1)}, f32[768]{0:T(1024)}, u32[]{:S(2)}) copy-start(f32[768]{0:T(1024)} %copy-done.29) | copy-start | bytes 9220
  772.2 56.2 %copy-start.34 = (f32[768]{0:T(1024)S(1)}, f32[768]{0:T(1024)}, u32[]{:S(2)}) copy-start(f32[768]{0:T(1024)} %param.27) | copy-start | bytes 9220
  772.2 56.2 %copy-start.61 = (f32[768]{0:T(1024)S(1)}, f32[768]{0:T(1024)}, u32[]{:S(2)}) copy-start(f32[768]{0:T(1024)} %param.28) | copy-start | bytes 9220
  772.3 664.4 %reduce-scatter.25.cloned.1.call-start = ((), (), s32[]{:S(2)}) async-start(), calls=%async_computation.16 | async-start | bytes 7962624 | tf_op jit(solution)/shard_map/reduce_scatter | solution.py:284
  836.8 621.6 %reduce-scatter.43.cloned.1.call-start = ((), (), s32[]{:S(2)}) async-start(), calls=%async_computation.26 | async-start | bytes 245760
  904.4 577.0 %reduce-scatter.39.cloned.1.call-start = ((), (), s32[]{:S(2)}) async-start(), calls=%async_computation.24 | async-start | bytes 245760
  975.9 588.3 %reduce-scatter.41.cloned.1.call-start = ((), (), s32[]{:S(2)}) async-start(), calls=%async_computation.25 | async-start | bytes 737280
  1143.0 298.1 %copy-start.27 = (f32[768]{0:T(1024)S(1)}, f32[768]{0:T(1024)}, u32[]{:S(2)}) copy-start(f32[768]{0:T(1024)} %copy-done.26) | copy-start | bytes 9220
  1143.0 298.1 %copy-start.28 = (f32[768]{0:T(1024)S(1)}, f32[768]{0:T(1024)}, u32[]{:S(2)}) copy-start(f32[768]{0:T(1024)} %get-tuple-element.447) | copy-start | bytes 9220
  1143.0 424.6 %reduce-scatter.31.cloned.1.call-start = ((), (), s32[]{:S(2)}) async-start(), calls=%async_computation.19 | async-start | bytes 737280 | tf_op jit(solution)/shard_map/reduce_scatter | solution.py:306
  1307.0 262.3 %reduce-scatter.37.cloned.1.call-start = ((), (), s32[]{:S(2)}) async-start(), calls=%async_computation.23 | async-start | bytes 737280
  1440.8 224.3 %all-gather.10.cloned.1.call-start = ((), (), s32[]{:S(2)}) async-start(), calls=%async_computation.22 | async-start | bytes 15409152 | tf_op jit(solution)/shard_map/all_gather | solution.py:217
  1497.9 51.2 %copy-start.36 = (f32[768]{0:T(1024)S(1)}, f32[768]{0:T(1024)}, u32[]{:S(2)}) copy-start(f32[768]{0:T(1024)} %param.27) | copy-start | bytes 9220
  1572.6 100.8 %copy-start.46 = (f32[150]{0:T(256)S(1)}, f32[150]{0:T(256)}, u32[]{:S(2)}) copy-start(f32[150]{0:T(256)} %copy-done.45) | copy-start | bytes 1804
  1572.6 100.8 %copy-start.41 = (f32[150]{0:T(256)S(1)}, f32[150]{0:T(256)}, u32[]{:S(2)}) copy-start(f32[150]{0:T(256)} %copy-done.40) | copy-start | bytes 1804
  (72 other events, 370.0 us)
Sparse Core Ops, SparseCore 0:
  19.2 40.1 all-gather.7
  60.9 37.4 all-gather.5
  730.1 47.8 reduce-scatter.20
  780.5 47.8 reduce-scatter.22
  831.8 69.1 reduce-scatter.34
  904.3 68.0 reduce-scatter.26
  976.1 162.5 reduce-scatter.32
  1142.2 162.5 reduce-scatter.28
  1308.5 128.0 reduce-scatter.24
  1439.7 18.7 reduce-scatter.42
  1461.6 19.6 reduce-scatter.38
  1483.9 22.0 reduce-scatter.40
  1508.7 22.0 reduce-scatter.30
  1533.3 22.0 reduce-scatter.36
  1558.5 106.5 all-gather.9
